TPU v7x, 1024 devices: a whole 4x4x32 slice. The times are simulated.
1024 devices in a mesh: dp: 16 (over x, y), expert: 64 (over z, core).
Axes of the slice: x: 4, y: 4, z: 32, core: 2. Of those that a mesh axis runs over, the one named last changes fastest.
Arguments:
- grad_out: bfloat16 [2048, 4096], P('expert', 'dp'), may hold values from -6 to 6
- routes: int32 [2048, 8], P('expert'), may hold values from 0 to 63, all different within a row; in each aligned block of 32 rows (0 to 31, 32 to 63, ...) at most 8 rows name the same one
- route_weight: float32 [2048, 8], P('expert'), may hold values from 0.2 to 1
- saved_input: bfloat16 [64, 512, 4096], P('expert', None, 'dp'), may hold values from -6 to 6
- saved_gate: bfloat16 [64, 512, 1024], P('expert'), may hold values from -6 to 6
- saved_up: bfloat16 [64, 512, 1024], P('expert'), may hold values from -6 to 6
- w_gate: bfloat16 [64, 4096, 1024], P('expert', 'dp'), may hold values from -0.09375 to 0.09375
- w_up: bfloat16 [64, 4096, 1024], P('expert', 'dp'), may hold values from -0.09375 to 0.09375
- w_down: bfloat16 [64, 1024, 4096], P('expert', None, 'dp'), may hold values from -0.1875 to 0.1875
Outputs:
- grad_in: bfloat16 [2048, 4096], P('expert', 'dp')
- grad_gate: bfloat16 [64, 4096, 1024], P('expert', 'dp')
- grad_up: bfloat16 [64, 4096, 1024], P('expert', 'dp')
- grad_down: bfloat16 [64, 1024, 4096], P('expert', None, 'dp')
Inputs may be any that keep to these rules, and one draw needn't show every extreme that they name: `routes`: each token names 8 different experts. Among the tokens of one block of 32 no expert is named by more than 8 tokens, and in every draw some expert is named by exactly 8 tokens of some block.
All inputs are finite; a program needn't handle non-finite values.
Results may differ from a plain program's by a relative error of at most 0.023.
Values may be sent and summed in bfloat16 or wider, within the bound.
A program may use at most 32 MiB of HBM per device.

v0:
```python
import jax
import jax.numpy as jnp
from jax import lax
from jax.sharding import PartitionSpec as P


def swiglu_grads(hidden_grad, gate_full, up_full):
    sigmoid_g = jax.nn.sigmoid(gate_full)
    d_gate = (hidden_grad * up_full * sigmoid_g * (1.0 + gate_full * (1.0 - sigmoid_g))).astype(
        jnp.bfloat16
    )
    d_up = (hidden_grad * gate_full * sigmoid_g).astype(jnp.bfloat16)
    return (d_gate, d_up)


def on_device(
    grad_out, routes, route_weight, saved_input, saved_gate, saved_up, w_gate, w_up, w_down
):
    experts = lax.axis_size("expert")
    tok_rows, columns = grad_out.shape
    top_count = routes.shape[1]
    capacity = saved_input.shape[1] // experts
    flat_routes = routes.reshape(-1)
    onehot = (flat_routes[:, None] == jnp.arange(experts, dtype=jnp.int32)[None, :]).astype(
        jnp.int32
    )
    before = jnp.cumsum(onehot, axis=0) - onehot
    ranks = jnp.sum(before * onehot, axis=1)
    targets = flat_routes * capacity + ranks
    scaled = (route_weight[:, :, None] * grad_out[:, None, :].astype(jnp.float32)).astype(
        jnp.bfloat16
    )
    outgoing = (
        jnp.zeros((experts * capacity, columns), jnp.bfloat16)
        .at[targets]
        .set(scaled.reshape(-1, columns))
    )
    incoming = lax.all_to_all(
        outgoing.reshape(experts, capacity, columns),
        "expert",
        split_axis=0,
        concat_axis=0,
        tiled=True,
    )
    slot_grads = incoming.reshape(experts * capacity, columns)
    contract_last = (((1,), (1,)), ((), ()))
    contract_first = (((0,), (0,)), ((), ()))
    partial_grad = lax.dot_general(
        slot_grads, w_down[0], contract_last, preferred_element_type=jnp.float32
    )
    gate_full = saved_gate[0].astype(jnp.float32)
    up_full = saved_up[0].astype(jnp.float32)
    hidden = (gate_full * jax.nn.sigmoid(gate_full) * up_full).astype(jnp.bfloat16)
    hidden_grad = lax.psum(partial_grad.astype(jnp.bfloat16), "dp").astype(jnp.float32)
    d_gate, d_up = swiglu_grads(hidden_grad, gate_full, up_full)
    slot_input = (
        lax.dot_general(d_gate, w_gate[0], contract_last, preferred_element_type=jnp.float32)
        + lax.dot_general(d_up, w_up[0], contract_last, preferred_element_type=jnp.float32)
    ).astype(jnp.bfloat16)
    inputs = saved_input[0]
    grad_gate = lax.dot_general(
        inputs, d_gate, contract_first, preferred_element_type=jnp.float32
    ).astype(jnp.bfloat16)
    grad_up = lax.dot_general(
        inputs, d_up, contract_first, preferred_element_type=jnp.float32
    ).astype(jnp.bfloat16)
    grad_down = lax.dot_general(
        hidden, slot_grads, contract_first, preferred_element_type=jnp.float32
    ).astype(jnp.bfloat16)
    returned = lax.all_to_all(
        slot_input.reshape(experts, capacity, columns),
        "expert",
        split_axis=0,
        concat_axis=0,
        tiled=True,
    )
    picked = returned.reshape(experts * capacity, columns)[targets].astype(jnp.float32)
    grad_in = jnp.sum(picked.reshape(tok_rows, top_count, columns), axis=1).astype(jnp.bfloat16)
    return (grad_in, grad_gate[None], grad_up[None], grad_down[None])


def solution(mesh):
    in_specs = (
        P("expert", "dp"),
        P("expert", None),
        P("expert", None),
        P("expert", None, "dp"),
        P("expert", None, None),
        P("expert", None, None),
        P("expert", "dp", None),
        P("expert", "dp", None),
        P("expert", None, "dp"),
    )
    out_specs = (
        P("expert", "dp"),
        P("expert", "dp", None),
        P("expert", "dp", None),
        P("expert", None, "dp"),
    )
    return jax.shard_map(
        on_device, mesh=mesh, in_specs=in_specs, out_specs=out_specs, check_vma=False
    )
```

profile of v0, /device:TPU:6, one launch (start us, length us, event | category | flops | bytes accessed | tf_op | source)
XLA Modules:
  0.0 307.4 jit_solution(10823135433960988795)
XLA Ops:
  7.2 0.0 copy-start
  7.2 0.0 all-reduce.2.cloned.1.call-start
  7.2 0.8 copy.16
  8.0 0.1 eq.29
  8.1 0.1 eq.25
  8.2 0.7 broadcast_multiply_fusion
  8.9 0.6 reduce-window.6
  9.5 0.2 slice_reduce_fusion
  9.8 0.1 copy.15
  9.8 0.1 mul.65
  9.9 0.7 convert_element_type.74
  10.7 0.8 copy.19
  11.4 0.1 mul.67
  11.5 0.1 fusion.39
  11.6 1.6 scatter_custom_fusion
  13.3 72.2 %all_to_all.10 = bf16[64,8,256]{2,1,0:T(8,128)(2,1)S(1)} all-to-all(bf16[64,8,256]{2,1,0:T(8,128)(2,1)S(1)} %bitcast.99), channel_id=1, replica_groups=mesh['dp'=16,'expert'=64] {'expert'}, dimensions={0} | all-to-all | bytes 524288 | tf_op jit(solution)/shard_map/all_to_all | solution.py:38
  85.5 1.5 convolution_convert_fusion
  87.0 0.0 all-reduce.2.cloned.1.call-update
  87.0 139.9 %all-reduce.2.cloned.1.call-done = bf16[512,1024]{1,0:T(8,128)(2,1)} async-done(((bf16[512,1024]{1,0:T(8,128)(2,1)}), bf16[512,1024]{1,0:T(8,128)(2,1)}) %all-reduce.2.cloned.1.call-update) | async-done | bytes 1048592 | tf_op jit(solution)/shard_map/psum | solution.py:54
  226.9 3.0 fusion.12
  229.9 0.5 fusion.24
  230.4 0.5 copy-done.2
  231.0 1.2 fusion.20
  232.1 23.5 %all-to-all-start.1 = ((bf16[64,8,256]{2,1,0:T(8,128)(2,1)}), bf16[64,8,256]{2,1,0:T(8,128)(2,1)S(1)}, u32[]{:S(2)}, u32[]{:S(2)}) async-start(bf16[64,8,256]{2,1,0:T(8,128)(2,1)} %fusion.20), calls=%async_computation.1 | async-start | bytes 524288 | tf_op jit(solution)/shard_map/all_to_all | solution.py:70
  255.7 3.4 %fusion.18 = bf16[1,1024,256]{2,1,0:T(8,128)(2,1)} fusion(bf16[1,512,1024]{2,1,0:T(8,128)(2,1)} %param.14, bf16[1,512,1024]{2,1,0:T(8,128)(2,1)} %param.13, bf16[64,8,256]{2,1,0:T(8,128)(2,1)S(1)} %all_to_all.10), kind=kOutput, calls=%fused_computation.31 | convolution fusion | flops 272891904 | bytes 2883584 | tf_op jit(solution)/shard_map/dot_general | solution.py:67
  259.1 0.5 fusion.16
  259.6 1.0 copy.20
  260.6 0.5 fusion.17
  261.1 1.0 copy.21
  262.1 36.6 %all-to-all-done.1 = bf16[64,8,256]{2,1,0:T(8,128)(2,1)S(1)} async-done(((bf16[64,8,256]{2,1,0:T(8,128)(2,1)}), bf16[64,8,256]{2,1,0:T(8,128)(2,1)S(1)}, u32[]{:S(2)}, u32[]{:S(2)}) %all-to-all-start.1) | async-done | bytes 262176 | tf_op jit(solution)/shard_map/all_to_all | solution.py:70
  298.7 1.2 gather_fusion
  299.9 0.7 bitcast_reduce_fusion
  (13 shorter events, 0.1 us)
Async XLA Ops:
  7.2 78.3 %copy-start = (bf16[1,1024,256]{2,1,0:T(8,128)(2,1)S(1)}, bf16[1,1024,256]{2,1,0:T(8,128)(2,1)}, u32[]{:S(2)}) copy-start(bf16[1,1024,256]{2,1,0:T(8,128)(2,1)} %param.17) | copy-start | bytes 1572868
  7.2 219.7 %all-reduce.2.cloned.1.call-start = ((), (), s32[]{:S(2)}) async-start(), calls=%async_computation.2 | async-start | bytes 2097152 | tf_op jit(solution)/shard_map/psum | solution.py:54
  226.9 3.0 copy-start.1
  229.9 1.0 copy-start.2
  232.1 66.6 %all-to-all-start.1 = ((bf16[64,8,256]{2,1,0:T(8,128)(2,1)}), bf16[64,8,256]{2,1,0:T(8,128)(2,1)S(1)}, u32[]{:S(2)}, u32[]{:S(2)}) async-start(bf16[64,8,256]{2,1,0:T(8,128)(2,1)} %fusion.20), calls=%async_computation.1 | async-start | bytes 524288 | tf_op jit(solution)/shard_map/all_to_all | solution.py:70
  255.7 3.4 %copy-start.3 = (bf16[1,512,256]{2,1,0:T(8,128)(2,1)S(1)}, bf16[1,512,256]{2,1,0:T(8,128)(2,1)}, u32[]{:S(2)}) copy-start(bf16[1,512,256]{2,1,0:T(8,128)(2,1)} %param.12) | copy-start | bytes 786436
  259.6 1.0 copy-start.4
Sparse Core Ops, SparseCore 0:
  87.1 139.7 all-reduce.1
where the time goes:
time: 308 us; the launch traced here: 307 us
  waiting for transfers between devices  177 us (57%)
  blocking collectives  72.2 us (23%)
  starting transfers between devices  23.6 us (8%)
  between operations  14.1 us (5%)
  other arithmetic  7.52 us (2%)
  matrix products  7.52 us (2%)
  local copies, waits for them, and re-layouts  5.93 us (2%)
    psum x1, waiting for transfers between devices, on_device(): lax.psum(partial_grad.astype(jnp.bfloat16), 'dp').astype(jnp.float32)  140 us
    all_to_all x1, blocking collectives, on_device(): lax.all_to_all(outgoing.reshape(experts, capacity, columns), 'expert', sp...  72.2 us
    all_to_all x1, waiting for transfers between devices, on_device(): lax.all_to_all(slot_input.reshape(experts, capacity, columns), 'expert',...  36.6 us
    all_to_all x1, starting transfers between devices, on_device(): lax.all_to_all(slot_input.reshape(experts, capacity, columns), 'expert',...  23.5 us
  transfers between devices with their start and end apart: 2, of which 2 were waited for; matrix products, arithmetic and copies ran while one was open for 2% of the time, Pallas kernels for 0%

commit v1 on v0

v1 whole, which is shorter than its diff:
```python
import jax
import jax.numpy as jnp
from jax import lax
from jax.experimental import pallas as pl
from jax.experimental.pallas import tpu as pltpu
from jax.sharding import PartitionSpec as P

MESH = pl.DeviceIdType.MESH
F32 = jnp.float32
BF16 = jnp.bfloat16

CHUNKS = (
    (0, 1, -1, 2, -2, 3, -3, 6),
    (-6, 4, 5, 7, 8, 9, -4, -5),
    (-7, -8, -9, 12, -12, 10, 11, 13),
    (14, 15, 16, -10, -11, -13, -14, -15),
)
ORDER = tuple(o for chunk in CHUNKS for o in chunk)
PLACE = {o: i for i, o in enumerate(ORDER)}
TREE = {
    0: (6, -6, 3, -3, 2, -2, 1, -1),
    6: (12, 9, 8, 7, 5, 4),
    -6: (-12, -9, -8, -7, -5, -4),
    12: (16, 15, 14, 13, 11, 10),
    -12: (-15, -14, -13, -11, -10),
}
PARENT = {o: k for k, kids in TREE.items() for o in kids}
NEAR = (1, -1, 2, -2, 3, -3, 4, -4, 6, -6)
NCH = len(CHUNKS)
LAST = (((1,), (1,)), ((), ()))
FIRST = (((0,), (0,)), ((), ()))


def kernel(
    n_dp,
    n_z,
    tok_ref,
    meta_ref,
    xin_ref,
    gate_ref,
    up_ref,
    wg_ref,
    wu_ref,
    wd_ref,
    gin_out,
    gg_out,
    gu_out,
    gd_out,
    buf,
    xin,
    gate,
    up,
    wg,
    wu,
    wd,
    fac_a,
    fac_b,
    hid,
    sel,
    sg,
    part,
    rsr,
    hg,
    dg,
    du,
    contr,
    sb,
    ssum,
    rb,
    gin,
    gg,
    gu,
    gd,
    lsem,
    osem,
    zs,
    zr,
    bs,
    br,
    rss,
    rsrs,
    ags,
    agr,
    cs,
    cr,
    zs2,
    zr2,
):
    d = lax.axis_index("dp")
    e = lax.axis_index("expert")
    z = e // 2
    c = e % 2
    x = d // 4
    y = d % 4

    def chip(o):
        return (d, ((z + (o + n_z)) % n_z) * 2 + c)

    sibling = (d, z * 2 + (1 - c))

    def peer(j):
        return (((x + j // 4) % 4) * 4 + (y + j % 4) % 4, e)

    def remote(src, dst, s, r, dev):
        return pltpu.make_async_remote_copy(
            src_ref=src, dst_ref=dst, send_sem=s, recv_sem=r, device_id=dev, device_id_type=MESH
        )

    barrier = pltpu.get_barrier_semaphore()
    for o in (6, -6, 4, -4, 3, -3, 2, -2, 1, -1):
        pl.semaphore_signal(barrier, inc=1, device_id=chip(o), device_id_type=MESH)
    for j in range(1, n_dp):
        pl.semaphore_signal(barrier, inc=1, device_id=peer(j), device_id_type=MESH)
    pl.semaphore_signal(barrier, inc=1, device_id=sibling, device_id_type=MESH)

    own = [
        pltpu.make_async_copy(tok_ref.at[:, pl.ds(0, 128)], buf.at[0, c, pl.ds(0, 32)], lsem.at[0]),
        pltpu.make_async_copy(tok_ref.at[:, pl.ds(128, 128)], buf.at[0, c, pl.ds(32, 32)], lsem.at[1]),
        pltpu.make_async_copy(meta_ref, buf.at[0, c, pl.ds(64, 16)], lsem.at[2]),
    ]
    for cp in own:
        cp.start()
    for i, o in enumerate(ORDER):
        rows = pl.ds(pl.multiple_of(((z + (o + n_z)) % n_z) * 16, 16), 16)
        pltpu.make_async_copy(gate_ref.at[rows], gate.at[pl.ds(16 * i, 16)], lsem.at[3]).start()
        pltpu.make_async_copy(up_ref.at[rows], up.at[pl.ds(16 * i, 16)], lsem.at[4]).start()
        pltpu.make_async_copy(xin_ref.at[rows], xin.at[pl.ds(16 * i, 16)], lsem.at[5]).start()
    load_wd = pltpu.make_async_copy(wd_ref, wd, lsem.at[6])
    load_wg = pltpu.make_async_copy(wg_ref, wg, lsem.at[7])
    load_wu = pltpu.make_async_copy(wu_ref, wu, lsem.at[8])
    load_wd.start()
    load_wg.start()
    load_wu.start()
    for cp in own:
        cp.wait()
    pl.semaphore_wait(barrier, len(NEAR) + n_dp)

    def hop(o):
        k = PARENT[o]
        i = PLACE[o]
        return remote(buf.at[PLACE[k], c], buf.at[i, c], zs.at[i], zr.at[i], chip(k - o))

    def relay(k):
        for o in TREE[k]:
            hop(o).start()

    def share(g):
        block = buf.at[pl.ds(8 * g, 8), c]
        return remote(block, block, bs.at[g], br.at[g], sibling)

    def arrived(g, skip=()):
        for o in CHUNKS[g]:
            if o not in skip:
                hop(o).wait_recv()

    relay(0)

    pltpu.make_async_copy(gate_ref, gate, lsem.at[3]).wait()
    pltpu.make_async_copy(up_ref, up, lsem.at[4]).wait()

    @pl.loop(0, 32)
    def _(i):
        rows = pl.ds(pl.multiple_of(i * 16, 16), 16)
        g32 = gate[rows, :].astype(F32)
        u32 = up[rows, :].astype(F32)
        s = 1.0 / (1.0 + jnp.exp(-g32))
        silu = g32 * s
        fac_b[rows, :] = silu
        fac_a[rows, :] = u32 * s * (1.0 + g32 * (1.0 - s))
        hid[rows, :] = (silu * u32).astype(BF16)

    line = lax.broadcasted_iota(jnp.int32, (128, 768), 0)
    lane = lax.broadcasted_iota(jnp.int32, (128, 768), 1)
    tok_of = lane & 31
    kind = lane >> 8
    spread = (
        ((kind == 0) & (line < tok_of))
        | ((kind == 1) & (line == tok_of))
        | ((kind == 2) & (line >= 32) & ((line & 31) == tok_of))
    )
    spread = jnp.where(spread, 1.0, 0.0).astype(BF16)
    e32 = e.astype(F32)
    load_wd.wait()

    def scatter(g):
        tags = buf[pl.ds(8 * g, 8), :, pl.ds(64, 16), :].reshape(16, 16, 128).astype(F32)
        hit = tags[:, 0:8, :] == e32
        found = jnp.sum(jnp.where(hit, tags[:, 8:16, :], 0.0), axis=1)
        wide = jnp.dot(found.astype(BF16), spread, preferred_element_type=F32)
        row8 = lax.broadcasted_iota(jnp.int32, (8, 768), 0)
        lane8 = lax.broadcasted_iota(jnp.int32, (8, 768), 1)
        mine = ((lane8 & 255) >> 5) == row8
        for q in range(2):
            flat = jnp.sum(jnp.where(mine, wide[8 * q : 8 * q + 8, :], 0.0), axis=0, keepdims=True)
            rank = flat[:, 0:256]
            there = flat[:, 256:512]
            weight = flat[:, 512:768]
            group = (lax.broadcasted_iota(jnp.int32, (1, 256), 1) >> 5) * 8
            key = jnp.where(there > 0.5, group.astype(F32) + rank, -1.0)
            slot = lax.broadcasted_iota(jnp.int32, (64, 256), 0).astype(F32)
            pick = slot == key
            scale = jnp.sum(jnp.where(pick, weight, 0.0), axis=1, keepdims=True)
            one = jnp.where(pick, 1.0, 0.0).astype(BF16)
            sel[2 * g + q] = one
            base = 8 * g + 4 * q
            low = buf[pl.ds(base, 4), :, pl.ds(0, 32), :].reshape(256, 128)
            high = buf[pl.ds(base, 4), :, pl.ds(32, 32), :].reshape(256, 128)
            rows = pl.ds(16 * base, 64)
            sg[rows, 0:128] = (jnp.dot(one, low, preferred_element_type=F32) * scale).astype(BF16)
            sg[rows, 128:256] = (jnp.dot(one, high, preferred_element_type=F32) * scale).astype(BF16)
        grads = sg[pl.ds(128 * g, 128), :]
        for h in range(2):
            sums = lax.dot_general(grads, wd[pl.ds(512 * h, 512), :], LAST, preferred_element_type=F32)
            part[g, :, h] = sums.astype(BF16).reshape(8, 16, 512)

    def rs(g, j):
        dev = peer(j)
        p = dev[0]
        return remote(part.at[g, p // 2, p % 2], rsr.at[g, j], rss.at[g, j], rsrs.at[g, j], dev)

    def ag(g, j):
        piece = hg.at[g, d // 2, d % 2]
        return remote(piece, piece, ags.at[g, j], agr.at[g, j], peer(j))

    def rs_start(g):
        @pl.loop(1, n_dp)
        def _(j):
            rs(g, j).start()

    def reduce(g):
        @pl.loop(1, n_dp)
        def _(j):
            rs(g, j).wait_recv()

        total = part[g, d // 2, d % 2].astype(F32)
        for j in range(1, n_dp):
            total = total + rsr[g, j].astype(F32)
        hg[g, d // 2, d % 2] = total.astype(BF16)

        @pl.loop(1, n_dp)
        def _(j):
            ag(g, j).start()

    def local(g):
        @pl.loop(1, n_dp)
        def _(j):
            ag(g, j).wait_recv()

        rows = pl.ds(128 * g, 128)
        for h in range(2):
            cols = pl.ds(512 * h, 512)
            grad = hg[g, :, h].reshape(128, 512).astype(F32)
            dg[rows, cols] = (grad * fac_a[rows, cols]).astype(BF16)
            du[rows, cols] = (grad * fac_b[rows, cols]).astype(BF16)
        out = lax.dot_general(dg[rows, :], wg[...], LAST, preferred_element_type=F32)
        out = out + lax.dot_general(du[rows, :], wu[...], LAST, preferred_element_type=F32)
        out = out.astype(BF16)
        for q in range(2):
            dense = lax.dot_general(
                sel[2 * g + q], out[64 * q : 64 * q + 64, :], FIRST, preferred_element_type=F32
            )
            contr[pl.ds(8 * g + 4 * q, 4)] = dense.astype(BF16).reshape(4, 2, 32, 256)
        pair(g).start()

    def pair(g):
        block = pl.ds(8 * g, 8)
        return remote(contr.at[block, 1 - c], sb.at[block], cs.at[g], cr.at[g], sibling)

    def back(o):
        k = PARENT[o]
        i = PLACE[o]
        return remote(ssum.at[i], rb.at[i], zs2.at[i], zr2.at[i], chip(o - k))

    def join(g):
        pair(g).wait_recv()
        block = pl.ds(8 * g, 8)
        ssum[block] = (contr[block, c].astype(F32) + sb[block].astype(F32)).astype(BF16)
        for o in CHUNKS[g]:
            if o not in TREE:
                back(o).start()

    def gather(k):
        total = ssum[PLACE[k]].astype(F32)
        for o in TREE[k][::-1]:
            back(o).wait_recv()
            total = total + rb[PLACE[o]].astype(F32)
        return total

    hop(6).wait_recv()
    relay(6)
    hop(-6).wait_recv()
    relay(-6)
    for o in CHUNKS[0]:
        if o not in TREE:
            hop(o).wait_recv()
    share(0).start()
    share(0).wait_recv()
    scatter(0)
    rs_start(0)
    for o in CHUNKS[1]:
        if o not in TREE:
            hop(o).wait_recv()
    share(1).start()
    hop(12).wait_recv()
    relay(12)
    hop(-12).wait_recv()
    relay(-12)
    share(1).wait_recv()
    scatter(1)
    rs_start(1)
    reduce(0)
    for g in (2, 3):
        for o in CHUNKS[g]:
            if o not in TREE:
                hop(o).wait_recv()
        share(g).start()
    for g in (2, 3):
        share(g).wait_recv()
        scatter(g)
        rs_start(g)
    reduce(1)
    load_wg.wait()
    load_wu.wait()
    local(0)
    reduce(2)
    reduce(3)
    local(1)
    join(0)
    local(2)
    join(1)
    local(3)
    join(2)
    join(3)
    for k in (12, -12):
        ssum[PLACE[k]] = gather(k).astype(BF16)
        back(k).start()

    pltpu.make_async_copy(xin_ref, xin, lsem.at[5]).wait()

    @pl.loop(0, 4)
    def _(i):
        cols = pl.ds(pl.multiple_of(i * 256, 256), 256)
        gg[:, cols] = lax.dot_general(
            xin[...], dg[:, cols], FIRST, preferred_element_type=F32
        ).astype(BF16)
        gu[:, cols] = lax.dot_general(
            xin[...], du[:, cols], FIRST, preferred_element_type=F32
        ).astype(BF16)
        gd[cols, :] = lax.dot_general(
            hid[:, cols], sg[...], FIRST, preferred_element_type=F32
        ).astype(BF16)

    outs = [
        pltpu.make_async_copy(gg, gg_out, osem.at[0]),
        pltpu.make_async_copy(gu, gu_out, osem.at[1]),
        pltpu.make_async_copy(gd, gd_out, osem.at[2]),
    ]
    for cp in outs:
        cp.start()
    for k in (6, -6):
        ssum[PLACE[k]] = gather(k).astype(BF16)
        back(k).start()
    gin[...] = gather(0).astype(BF16)
    last = pltpu.make_async_copy(gin, gin_out, osem.at[3])
    last.start()

    for o in ORDER:
        if o != 0:
            hop(o).wait_send()
            back(o).wait_send()
    for g in range(NCH):
        share(g).wait_send()
        pair(g).wait_send()

        @pl.loop(1, n_dp)
        def _(j):
            rs(g, j).wait_send()
            ag(g, j).wait_send()

    for cp in outs:
        cp.wait()
    last.wait()


def solution(mesh):
    n_dp = mesh.shape["dp"]
    n_z = mesh.shape["expert"] // 2

    def on_device(grad_out, routes, route_weight, saved_input, saved_gate, saved_up, w_gate, w_up, w_down):
        named = jnp.tile(routes.T.astype(F32), (1, 4))
        w = route_weight.T
        top = lax.reduce_precision(w, 8, 7)
        rest = w - top
        mid = lax.reduce_precision(rest, 8, 7)
        low = rest - mid
        values = jnp.concatenate([jnp.ones_like(w), top, mid, low], axis=1)
        meta = jnp.concatenate([named, values], axis=0).astype(BF16)
        anywhere = pl.BlockSpec(memory_space=pl.ANY)
        dma = pltpu.SemaphoreType.DMA
        vm = pltpu.VMEM
        grads = pl.pallas_call(
            lambda *refs: kernel(n_dp, n_z, *refs),
            out_shape=(
                jax.ShapeDtypeStruct((32, 256), BF16),
                jax.ShapeDtypeStruct((256, 1024), BF16),
                jax.ShapeDtypeStruct((256, 1024), BF16),
                jax.ShapeDtypeStruct((1024, 256), BF16),
            ),
            in_specs=[anywhere] * 8,
            out_specs=[anywhere] * 4,
            scratch_shapes=[
                vm((32, 2, 80, 128), BF16),
                vm((512, 256), BF16),
                vm((512, 1024), BF16),
                vm((512, 1024), BF16),
                vm((256, 1024), BF16),
                vm((256, 1024), BF16),
                vm((1024, 256), BF16),
                vm((512, 1024), F32),
                vm((512, 1024), F32),
                vm((512, 1024), BF16),
                vm((8, 64, 256), BF16),
                vm((512, 256), BF16),
                vm((NCH, 8, 2, 16, 512), BF16),
                vm((NCH, 16, 16, 512), BF16),
                vm((NCH, 8, 2, 16, 512), BF16),
                vm((512, 1024), BF16),
                vm((512, 1024), BF16),
                vm((32, 2, 32, 256), BF16),
                vm((32, 32, 256), BF16),
                vm((32, 32, 256), BF16),
                vm((32, 32, 256), BF16),
                vm((32, 256), BF16),
                vm((256, 1024), BF16),
                vm((256, 1024), BF16),
                vm((1024, 256), BF16),
                dma((9,)),
                dma((4,)),
                dma((32,)),
                dma((32,)),
                dma((NCH,)),
                dma((NCH,)),
                dma((NCH, 16)),
                dma((NCH, 16)),
                dma((NCH, 16)),
                dma((NCH, 16)),
                dma((NCH,)),
                dma((NCH,)),
                dma((32,)),
                dma((32,)),
            ],
            name="expert_backward",
            compiler_params=pltpu.CompilerParams(
                collective_id=0, has_side_effects=True, vmem_limit_bytes=44 * 1024 * 1024
            ),
        )(
            grad_out,
            meta,
            saved_input[0],
            saved_gate[0],
            saved_up[0],
            w_gate[0],
            w_up[0],
            w_down[0],
        )
        grad_in, grad_gate, grad_up, grad_down = grads
        return (grad_in, grad_gate[None], grad_up[None], grad_down[None])

    in_specs = (
        P("expert", "dp"),
        P("expert", None),
        P("expert", None),
        P("expert", None, "dp"),
        P("expert", None, None),
        P("expert", None, None),
        P("expert", "dp", None),
        P("expert", "dp", None),
        P("expert", None, "dp"),
    )
    out_specs = (
        P("expert", "dp"),
        P("expert", "dp", None),
        P("expert", "dp", None),
        P("expert", None, "dp"),
    )
    return jax.shard_map(
        on_device, mesh=mesh, in_specs=in_specs, out_specs=out_specs, check_vma=False
    )
```

time: 308 us -> 103 us (0.33)
  waiting for transfers between devices: 177 us -> 0 us
  Pallas kernels: 0 us -> 89.7 us
  blocking collectives: 72.2 us -> 0 us
  starting transfers between devices: 23.6 us -> 0 us
  between operations: 14.1 us -> 0.67 us
  matrix products: 7.52 us -> 0 us
  other arithmetic: 7.52 us -> 0.09 us
  local copies, waits for them, and re-layouts: 5.93 us -> 11.5 us
    psum x1 -> x0, waiting for transfers between devices: 140 us -> none  [on_device(): lax.psum(partial_grad.astype(jnp.bfloat16), 'dp').astype(jnp.float32)]
    pallas_call x0 -> x1, Pallas kernels: none -> 89.7 us  [on_device(): pl.pallas_call(lambda *refs: kernel(n_dp, n_z, *refs), out_shape=(jax.Sha...]
    all_to_all x1 -> x0, blocking collectives: 72.2 us -> none  [on_device(): lax.all_to_all(outgoing.reshape(experts, capacity, columns), 'expert', sp...]
    all_to_all x1 -> x0, waiting for transfers between devices: 36.6 us -> none  [on_device(): lax.all_to_all(slot_input.reshape(experts, capacity, columns), 'expert',...]
    all_to_all x1 -> x0, starting transfers between devices: 23.5 us -> none  [on_device(): lax.all_to_all(slot_input.reshape(experts, capacity, columns), 'expert',...]
    dot_general x6 -> x0, matrix products: 7.52 us -> none  [the longest x1 3.4 us: on_device(): lax.dot_general(hidden, slot_grads, contract_first, preferred_element_typ...]
    unnamed x14 -> x22, local copies, waits for them, and re-layouts: 4.16 us -> 11.4 us
    convert_element_type x3 -> x0, other arithmetic: 3.76 us -> none  [the longest x1 3.02 us: swiglu_grads(): d_up = (hidden_grad * gate_full * sigmoid_g).astype(jnp.bfloat16)]
  transfers between devices with their start and end apart: 2 -> 0, of which waited for: 2 -> 0; matrix products, arithmetic and copies ran while one was open for 2% -> 0% of each run, Pallas kernels for 0% -> 0%
where the time goes in v1:
time: 103 us; the launch traced here: 102 us
  Pallas kernels  89.7 us (87%)
  local copies, waits for them, and re-layouts  11.5 us (11%)
    pallas_call x1, Pallas kernels, on_device(): pl.pallas_call(lambda *refs: kernel(n_dp, n_z, *refs), out_shape=(jax.Sha...  89.7 us
    unnamed x22, local copies, waits for them, and re-layouts  11.4 us

profile of v1, /device:TPU:6, one launch (start us, length us, event | category | flops | bytes accessed | tf_op | source)
XLA Modules:
  0.0 101.9 jit_solution(12174350898642073398)
XLA Ops:
  0.6 0.0 copy-start.7
  0.6 0.7 copy-done.7
  1.3 0.0 copy-start.8
  1.3 0.1 tile.11
  1.4 0.6 copy-done.8
  2.0 0.0 copy-start.6
  2.0 0.1 maximum_maximum_fusion.refs_1_
  2.1 0.6 copy-done.6
  2.7 0.0 copy-start
  2.7 1.2 %copy-done = bf16[1,512,1024]{2,1,0:T(8,128)(2,1)S(1)} copy-done((bf16[1,512,1024]{2,1,0:T(8,128)(2,1)S(1)}, bf16[1,512,1024]{2,1,0:T(8,128)(2,1)}, u32[]{:S(2)}) %copy-start) | copy-done | bytes 1048600
  4.0 0.0 copy-start.1
  4.0 1.2 %copy-done.1 = bf16[1,512,1024]{2,1,0:T(8,128)(2,1)S(1)} copy-done((bf16[1,512,1024]{2,1,0:T(8,128)(2,1)S(1)}, bf16[1,512,1024]{2,1,0:T(8,128)(2,1)}, u32[]{:S(2)}) %copy-start.1) | copy-done | bytes 1048600
  5.2 0.0 copy-start.2
  5.2 1.0 %copy-done.2 = bf16[1,256,1024]{2,1,0:T(8,128)(2,1)S(1)} copy-done((bf16[1,256,1024]{2,1,0:T(8,128)(2,1)S(1)}, bf16[1,256,1024]{2,1,0:T(8,128)(2,1)}, u32[]{:S(2)}) %copy-start.2) | copy-done | bytes 524312
  6.2 0.0 copy-start.3
  6.2 1.0 %copy-done.3 = bf16[1,256,1024]{2,1,0:T(8,128)(2,1)S(1)} copy-done((bf16[1,256,1024]{2,1,0:T(8,128)(2,1)S(1)}, bf16[1,256,1024]{2,1,0:T(8,128)(2,1)}, u32[]{:S(2)}) %copy-start.3) | copy-done | bytes 524312
  7.3 0.0 copy-start.4
  7.3 1.0 %copy-done.4 = bf16[1,1024,256]{2,1,0:T(8,128)(2,1)S(1)} copy-done((bf16[1,1024,256]{2,1,0:T(8,128)(2,1)S(1)}, bf16[1,1024,256]{2,1,0:T(8,128)(2,1)}, u32[]{:S(2)}) %copy-start.4) | copy-done | bytes 524312
  8.3 0.0 copy-start.5
  8.3 0.9 copy-done.5
  9.3 89.7 %expert_backward.1 = (bf16[32,256]{1,0:T(8,128)(2,1)S(1)}, bf16[256,1024]{1,0:T(8,128)(2,1)S(1)}, bf16[256,1024]{1,0:T(8,128)(2,1)S(1)}, bf16[1024,256]{1,0:T(8,128)(2,1)S(1)}) custom-call(bf16[32,256]{1,0:T(8,128)(2,1)S(1)} %copy-done.6, bf16[16,128]{1,0:T(8,128)(2,1)S(1)} %maximum_maximum_fusion.refs_1_, bf16[512,256]{1,0:T(8,128)(2,1)S(1)} %bitcast.26, ...), custom_call_target="tpu_custom_call" | custom-call | tf_op jit(solution)/shard_map/expert_backward/pallas_call | solution.py:401
  98.9 0.6 copy.17
  99.5 0.8 copy.18
  100.3 0.8 copy.19
  101.1 0.8 copy.20
  (4 shorter events, 0.0 us)
Async XLA Ops:
  0.6 0.7 copy-start.7
  1.3 0.7 copy-start.8
  2.0 0.7 copy-start.6
  2.7 1.2 %copy-start = (bf16[1,512,1024]{2,1,0:T(8,128)(2,1)S(1)}, bf16[1,512,1024]{2,1,0:T(8,128)(2,1)}, u32[]{:S(2)}) copy-start(bf16[1,512,1024]{2,1,0:T(8,128)(2,1)} %param.13) | copy-start | bytes 3145732
  4.0 1.2 %copy-start.1 = (bf16[1,512,1024]{2,1,0:T(8,128)(2,1)S(1)}, bf16[1,512,1024]{2,1,0:T(8,128)(2,1)}, u32[]{:S(2)}) copy-start(bf16[1,512,1024]{2,1,0:T(8,128)(2,1)} %param.14) | copy-start | bytes 3145732
  5.2 1.0 %copy-start.2 = (bf16[1,256,1024]{2,1,0:T(8,128)(2,1)S(1)}, bf16[1,256,1024]{2,1,0:T(8,128)(2,1)}, u32[]{:S(2)}) copy-start(bf16[1,256,1024]{2,1,0:T(8,128)(2,1)} %param.15) | copy-start | bytes 1572868
  6.2 1.0 %copy-start.3 = (bf16[1,256,1024]{2,1,0:T(8,128)(2,1)S(1)}, bf16[1,256,1024]{2,1,0:T(8,128)(2,1)}, u32[]{:S(2)}) copy-start(bf16[1,256,1024]{2,1,0:T(8,128)(2,1)} %param.16) | copy-start | bytes 1572868
  7.3 1.0 %copy-start.4 = (bf16[1,1024,256]{2,1,0:T(8,128)(2,1)S(1)}, bf16[1,1024,256]{2,1,0:T(8,128)(2,1)}, u32[]{:S(2)}) copy-start(bf16[1,1024,256]{2,1,0:T(8,128)(2,1)} %param.17) | copy-start | bytes 1572868
  8.3 0.9 copy-start.5

commit v2 on v1

--- a/solution.py
+++ b/solution.py
@@ -11,21 +11,31 @@
 
 CHUNKS = (
     (0, 1, -1, 2, -2, 3, -3, 6),
-    (-6, 4, 5, 7, 8, 9, -4, -5),
-    (-7, -8, -9, 12, -12, 10, 11, 13),
-    (14, 15, 16, -10, -11, -13, -14, -15),
+    (-6, 5, -5, 7, -7, 8, -8, 4),
+    (-4, 9, -9, 12, -12, 11, -11, 13),
+    (-13, 14, -14, 10, -10, 15, -15, 16),
 )
 ORDER = tuple(o for chunk in CHUNKS for o in chunk)
 PLACE = {o: i for i, o in enumerate(ORDER)}
 TREE = {
-    0: (6, -6, 3, -3, 2, -2, 1, -1),
-    6: (12, 9, 8, 7, 5, 4),
-    -6: (-12, -9, -8, -7, -5, -4),
-    12: (16, 15, 14, 13, 11, 10),
-    -12: (-15, -14, -13, -11, -10),
+    0: (6, -6, 2, -2, 1, -1),
+    2: (3,),
+    -2: (-3,),
+    6: (12, 8, 5, 7),
+    -6: (-12, -8, -5, -7),
+    5: (4,),
+    -5: (-4,),
+    8: (9,),
+    -8: (-9,),
+    12: (14, 11, 13),
+    -12: (-14, -11, -13),
+    14: (16, 15),
+    -14: (-15,),
+    11: (10,),
+    -11: (-10,),
 }
 PARENT = {o: k for k, kids in TREE.items() for o in kids}
-NEAR = (1, -1, 2, -2, 3, -3, 4, -4, 6, -6)
+NEAR = (6, -6, 2, -2, 1, -1)
 NCH = len(CHUNKS)
 LAST = (((1,), (1,)), ((), ()))
 FIRST = (((0,), (0,)), ((), ()))
@@ -35,7 +45,8 @@
     n_dp,
     n_z,
     tok_ref,
-    meta_ref,
+    named_ref,
+    weight_ref,
     xin_ref,
     gate_ref,
     up_ref,
@@ -47,6 +58,7 @@
     gu_out,
     gd_out,
     buf,
+    xin_by_chip,
     xin,
     gate,
     up,
@@ -96,6 +108,9 @@
     def chip(o):
         return (d, ((z + (o + n_z)) % n_z) * 2 + c)
 
+    def rows_of(o):
+        return pl.ds(pl.multiple_of(((z + (o + n_z)) % n_z) * 16, 16), 16)
+
     sibling = (d, z * 2 + (1 - c))
 
     def peer(j):
@@ -107,7 +122,7 @@
         )
 
     barrier = pltpu.get_barrier_semaphore()
-    for o in (6, -6, 4, -4, 3, -3, 2, -2, 1, -1):
+    for o in NEAR:
         pl.semaphore_signal(barrier, inc=1, device_id=chip(o), device_id_type=MESH)
     for j in range(1, n_dp):
         pl.semaphore_signal(barrier, inc=1, device_id=peer(j), device_id_type=MESH)
@@ -116,21 +131,36 @@
     own = [
         pltpu.make_async_copy(tok_ref.at[:, pl.ds(0, 128)], buf.at[0, c, pl.ds(0, 32)], lsem.at[0]),
         pltpu.make_async_copy(tok_ref.at[:, pl.ds(128, 128)], buf.at[0, c, pl.ds(32, 32)], lsem.at[1]),
-        pltpu.make_async_copy(meta_ref, buf.at[0, c, pl.ds(64, 16)], lsem.at[2]),
     ]
     for cp in own:
         cp.start()
-    for i, o in enumerate(ORDER):
-        rows = pl.ds(pl.multiple_of(((z + (o + n_z)) % n_z) * 16, 16), 16)
-        pltpu.make_async_copy(gate_ref.at[rows], gate.at[pl.ds(16 * i, 16)], lsem.at[3]).start()
-        pltpu.make_async_copy(up_ref.at[rows], up.at[pl.ds(16 * i, 16)], lsem.at[4]).start()
-        pltpu.make_async_copy(xin_ref.at[rows], xin.at[pl.ds(16 * i, 16)], lsem.at[5]).start()
+    load_gate = pltpu.make_async_copy(gate_ref, gate, lsem.at[3])
+    load_up = pltpu.make_async_copy(up_ref, up, lsem.at[4])
+    load_xin = pltpu.make_async_copy(xin_ref, xin_by_chip, lsem.at[5])
     load_wd = pltpu.make_async_copy(wd_ref, wd, lsem.at[6])
     load_wg = pltpu.make_async_copy(wg_ref, wg, lsem.at[7])
     load_wu = pltpu.make_async_copy(wu_ref, wu, lsem.at[8])
-    load_wd.start()
-    load_wg.start()
-    load_wu.start()
+    for cp in (load_gate, load_up, load_wd, load_wg, load_wu, load_xin):
+        cp.start()
+
+    token = lax.broadcasted_iota(jnp.int32, (32, 128), 0)
+    lane = lax.broadcasted_iota(jnp.int32, (32, 128), 1)
+    match = (lane & 31) == token
+
+    def lay(values, where):
+        copy = jnp.where(where, 1.0, 0.0).astype(BF16)
+        return jnp.dot(values, copy, preferred_element_type=F32)
+
+    weight = weight_ref[...]
+    top = weight.astype(BF16)
+    rest = weight - top.astype(F32)
+    mid = rest.astype(BF16)
+    low = (rest - mid.astype(F32)).astype(BF16)
+    kind = lane >> 5
+    names = lay(named_ref[...].astype(F32).astype(BF16), match)
+    terms = lay(top, match & (kind == 1)) + lay(mid, match & (kind == 2)) + lay(low, match & (kind == 3))
+    terms = jnp.where(lax.broadcasted_iota(jnp.int32, (8, 128), 1) < 32, 1.0, terms)
+    buf[0, c, 64:80, :] = jnp.concatenate([names, terms], axis=0).astype(BF16)
     for cp in own:
         cp.wait()
     pl.semaphore_wait(barrier, len(NEAR) + n_dp)
@@ -138,7 +168,7 @@
     def hop(o):
         k = PARENT[o]
         i = PLACE[o]
-        return remote(buf.at[PLACE[k], c], buf.at[i, c], zs.at[i], zr.at[i], chip(k - o))
+        return remote(buf.at[PLACE[k], c], buf.at[i, c], zs.at[0], zr.at[i], chip(k - o))
 
     def relay(k):
         for o in TREE[k]:
@@ -148,21 +178,15 @@
         block = buf.at[pl.ds(8 * g, 8), c]
         return remote(block, block, bs.at[g], br.at[g], sibling)
 
-    def arrived(g, skip=()):
-        for o in CHUNKS[g]:
-            if o not in skip:
-                hop(o).wait_recv()
-
     relay(0)
 
-    pltpu.make_async_copy(gate_ref, gate, lsem.at[3]).wait()
-    pltpu.make_async_copy(up_ref, up, lsem.at[4]).wait()
-
-    @pl.loop(0, 32)
-    def _(i):
-        rows = pl.ds(pl.multiple_of(i * 16, 16), 16)
-        g32 = gate[rows, :].astype(F32)
-        u32 = up[rows, :].astype(F32)
+    load_gate.wait()
+    load_up.wait()
+    for i, o in enumerate(ORDER):
+        there = rows_of(o)
+        rows = pl.ds(16 * i, 16)
+        g32 = gate[there, :].astype(F32)
+        u32 = up[there, :].astype(F32)
         s = 1.0 / (1.0 + jnp.exp(-g32))
         silu = g32 * s
         fac_b[rows, :] = silu
@@ -216,22 +240,27 @@
     def rs(g, j):
         dev = peer(j)
         p = dev[0]
-        return remote(part.at[g, p // 2, p % 2], rsr.at[g, j], rss.at[g, j], rsrs.at[g, j], dev)
+        return remote(part.at[g, p // 2, p % 2], rsr.at[g, j], rss.at[g], rsrs.at[g], dev)
 
     def ag(g, j):
         piece = hg.at[g, d // 2, d % 2]
-        return remote(piece, piece, ags.at[g, j], agr.at[g, j], peer(j))
+        return remote(piece, piece, ags.at[g], agr.at[g], peer(j))
 
     def rs_start(g):
         @pl.loop(1, n_dp)
         def _(j):
             rs(g, j).start()
 
+    def rs_all(g):
+        block = rsr.at[g, pl.ds(1, n_dp - 1)]
+        return remote(block, block, rss.at[g], rsrs.at[g], sibling)
+
+    def ag_all(g):
+        block = rsr.at[g, pl.ds(1, n_dp - 1)]
+        return remote(block, block, ags.at[g], agr.at[g], sibling)
+
     def reduce(g):
-        @pl.loop(1, n_dp)
-        def _(j):
-            rs(g, j).wait_recv()
-
+        rs_all(g).wait_recv()
         total = part[g, d // 2, d % 2].astype(F32)
         for j in range(1, n_dp):
             total = total + rsr[g, j].astype(F32)
@@ -242,10 +271,7 @@
             ag(g, j).start()
 
     def local(g):
-        @pl.loop(1, n_dp)
-        def _(j):
-            ag(g, j).wait_recv()
-
+        ag_all(g).wait_recv()
         rows = pl.ds(128 * g, 128)
         for h in range(2):
             cols = pl.ds(512 * h, 512)
@@ -269,7 +295,7 @@
     def back(o):
         k = PARENT[o]
         i = PLACE[o]
-        return remote(ssum.at[i], rb.at[i], zs2.at[i], zr2.at[i], chip(o - k))
+        return remote(ssum.at[i], rb.at[i], zs2.at[0], zr2.at[i], chip(o - k))
 
     def join(g):
         pair(g).wait_recv()
@@ -279,6 +305,11 @@
             if o not in TREE:
                 back(o).start()
 
+    def forward(*ks):
+        for k in ks:
+            ssum[PLACE[k]] = gather(k).astype(BF16)
+            back(k).start()
+
     def gather(k):
         total = ssum[PLACE[k]].astype(F32)
         for o in TREE[k][::-1]:
@@ -286,56 +317,57 @@
             total = total + rb[PLACE[o]].astype(F32)
         return total
 
-    hop(6).wait_recv()
-    relay(6)
-    hop(-6).wait_recv()
-    relay(-6)
-    for o in CHUNKS[0]:
-        if o not in TREE:
-            hop(o).wait_recv()
-    share(0).start()
-    share(0).wait_recv()
-    scatter(0)
-    rs_start(0)
-    for o in CHUNKS[1]:
-        if o not in TREE:
-            hop(o).wait_recv()
-    share(1).start()
-    hop(12).wait_recv()
-    relay(12)
-    hop(-12).wait_recv()
-    relay(-12)
-    share(1).wait_recv()
-    scatter(1)
-    rs_start(1)
-    reduce(0)
-    for g in (2, 3):
+    def pass_on(*ks):
+        for k in ks:
+            hop(k).wait_recv()
+            relay(k)
+
+    def leaves(g):
         for o in CHUNKS[g]:
             if o not in TREE:
                 hop(o).wait_recv()
         share(g).start()
-    for g in (2, 3):
-        share(g).wait_recv()
-        scatter(g)
-        rs_start(g)
+
+    pass_on(2, -2, 6, -6)
+    leaves(0)
+    share(0).wait_recv()
+    scatter(0)
+    rs_start(0)
+    pass_on(8, -8, 5, -5)
+    leaves(1)
+    pass_on(12, -12)
+    share(1).wait_recv()
+    scatter(1)
+    rs_start(1)
+    pass_on(14, -14, 11, -11)
+    leaves(2)
+    reduce(0)
+    share(2).wait_recv()
+    scatter(2)
+    rs_start(2)
+    leaves(3)
     reduce(1)
+    share(3).wait_recv()
+    scatter(3)
+    rs_start(3)
     load_wg.wait()
     load_wu.wait()
     local(0)
     reduce(2)
+    join(0)
+    local(1)
     reduce(3)
-    local(1)
-    join(0)
+    join(1)
     local(2)
-    join(1)
+    join(2)
     local(3)
-    join(2)
+    forward(5, -5, 8, -8, 2, -2)
     join(3)
-    for k in (12, -12):
-        ssum[PLACE[k]] = gather(k).astype(BF16)
-        back(k).start()
-
-    pltpu.make_async_copy(xin_ref, xin, lsem.at[5]).wait()
+    forward(14, -14, 11, -11, 12, -12)
+
+    load_xin.wait()
+    for i, o in enumerate(ORDER):
+        xin[pl.ds(16 * i, 16), :] = xin_by_chip[rows_of(o), :]
 
     @pl.loop(0, 4)
     def _(i):
@@ -357,44 +389,50 @@
     ]
     for cp in outs:
         cp.start()
-    for k in (6, -6):
-        ssum[PLACE[k]] = gather(k).astype(BF16)
-        back(k).start()
+    hops = buf.at[pl.ds(1, n_z - 1), c]
+    remote(hops, hops, zs.at[0], zr.at[0], sibling).wait_send()
+    for g in range(NCH):
+        share(g).wait_send()
+        pair(g).wait_send()
+        rs_all(g).wait_send()
+        ag_all(g).wait_send()
+    forward(6, -6)
     gin[...] = gather(0).astype(BF16)
     last = pltpu.make_async_copy(gin, gin_out, osem.at[3])
     last.start()
 
-    for o in ORDER:
-        if o != 0:
-            hop(o).wait_send()
-            back(o).wait_send()
-    for g in range(NCH):
-        share(g).wait_send()
-        pair(g).wait_send()
-
-        @pl.loop(1, n_dp)
-        def _(j):
-            rs(g, j).wait_send()
-            ag(g, j).wait_send()
-
+    hops = rb.at[pl.ds(1, n_z - 1)]
+    remote(hops, hops, zs2.at[0], zr2.at[0], sibling).wait_send()
     for cp in outs:
         cp.wait()
     last.wait()
 
 
+def hand_over(*refs):
+    sources, targets, held, sem = refs[:4], refs[4:8], refs[8:12], refs[12]
+    loads, stores = [], []
+    for i in range(4):
+        parts = 2 if i else 1
+        rows = sources[i].shape[0] // parts
+        for part in range(parts):
+            block = pl.ds(rows * part, rows)
+            here = held[i].at[block]
+            loads.append(pltpu.make_async_copy(sources[i].at[block], here, sem.at[0, i, part]))
+            stores.append(pltpu.make_async_copy(here, targets[i].at[block], sem.at[1, i, part]))
+    for load in loads:
+        load.start()
+    for load, store in zip(loads, stores):
+        load.wait()
+        store.start()
+    for store in stores:
+        store.wait()
+
+
 def solution(mesh):
     n_dp = mesh.shape["dp"]
     n_z = mesh.shape["expert"] // 2
 
     def on_device(grad_out, routes, route_weight, saved_input, saved_gate, saved_up, w_gate, w_up, w_down):
-        named = jnp.tile(routes.T.astype(F32), (1, 4))
-        w = route_weight.T
-        top = lax.reduce_precision(w, 8, 7)
-        rest = w - top
-        mid = lax.reduce_precision(rest, 8, 7)
-        low = rest - mid
-        values = jnp.concatenate([jnp.ones_like(w), top, mid, low], axis=1)
-        meta = jnp.concatenate([named, values], axis=0).astype(BF16)
         anywhere = pl.BlockSpec(memory_space=pl.ANY)
         dma = pltpu.SemaphoreType.DMA
         vm = pltpu.VMEM
@@ -406,10 +444,11 @@
                 jax.ShapeDtypeStruct((256, 1024), BF16),
                 jax.ShapeDtypeStruct((1024, 256), BF16),
             ),
-            in_specs=[anywhere] * 8,
+            in_specs=[anywhere] + [pl.BlockSpec(memory_space=pltpu.VMEM)] * 2 + [anywhere] * 6,
             out_specs=[anywhere] * 4,
             scratch_shapes=[
                 vm((32, 2, 80, 128), BF16),
+                vm((512, 256), BF16),
                 vm((512, 256), BF16),
                 vm((512, 1024), BF16),
                 vm((512, 1024), BF16),
@@ -436,26 +475,27 @@
                 vm((1024, 256), BF16),
                 dma((9,)),
                 dma((4,)),
+                dma((1,)),
                 dma((32,)),
-                dma((32,)),
-                dma((NCH,)),
-                dma((NCH,)),
-                dma((NCH, 16)),
-                dma((NCH, 16)),
-                dma((NCH, 16)),
-                dma((NCH, 16)),
-                dma((NCH,)),
-                dma((NCH,)),
-                dma((32,)),
+                dma((NCH,)),
+                dma((NCH,)),
+                dma((NCH,)),
+                dma((NCH,)),
+                dma((NCH,)),
+                dma((NCH,)),
+                dma((NCH,)),
+                dma((NCH,)),
+                dma((1,)),
                 dma((32,)),
             ],
             name="expert_backward",
             compiler_params=pltpu.CompilerParams(
-                collective_id=0, has_side_effects=True, vmem_limit_bytes=44 * 1024 * 1024
+                collective_id=0, has_side_effects=True, vmem_limit_bytes=56 * 1024 * 1024
             ),
         )(
             grad_out,
-            meta,
+            routes.T,
+            route_weight.T,
             saved_input[0],
             saved_gate[0],
             saved_up[0],
@@ -463,7 +503,15 @@
             w_up[0],
             w_down[0],
         )
-        grad_in, grad_gate, grad_up, grad_down = grads
+        grad_in, grad_gate, grad_up, grad_down = pl.pallas_call(
+            hand_over,
+            out_shape=tuple(jax.ShapeDtypeStruct(a.shape, a.dtype) for a in grads),
+            in_specs=[anywhere] * 4,
+            out_specs=[anywhere] * 4,
+            scratch_shapes=[vm(a.shape, a.dtype) for a in grads] + [dma((2, 4, 2))],
+            name="hand_over",
+            compiler_params=pltpu.CompilerParams(vmem_limit_bytes=56 * 1024 * 1024),
+        )(*grads)
         return (grad_in, grad_gate[None], grad_up[None], grad_down[None])
 
     in_specs = (

time: 103 us -> 92.8 us (0.901)
  local copies, waits for them, and re-layouts: 11.5 us -> 0 us
  Pallas kernels: 89.7 us -> 91 us
    unnamed x22 -> x0, local copies, waits for them, and re-layouts: 11.4 us -> none
    pallas_call x0 -> x1, Pallas kernels: none -> 2.24 us  [on_device(): pl.pallas_call(hand_over, out_shape=tuple((jax.ShapeDtypeStruct(a.shape,...]
where the time goes in v2:
time: 92.8 us; the launch traced here: 91.6 us
  Pallas kernels  91 us (98%)
    pallas_call x1, Pallas kernels, on_device(): pl.pallas_call(lambda *refs: kernel(n_dp, n_z, *refs), out_shape=(jax.Sha...  88.7 us
    pallas_call x1, Pallas kernels, on_device(): pl.pallas_call(hand_over, out_shape=tuple((jax.ShapeDtypeStruct(a.shape,...  2.24 us

profile of v2, /device:TPU:6, one launch (start us, length us, event | category | flops | bytes accessed | tf_op | source)
XLA Modules:
  0.0 91.6 jit_solution(16169332166289193532)
XLA Ops:
  0.6 88.7 %expert_backward.1 = (bf16[32,256]{1,0:T(8,128)(2,1)}, bf16[256,1024]{1,0:T(8,128)(2,1)}, bf16[256,1024]{1,0:T(8,128)(2,1)}, bf16[1024,256]{1,0:T(8,128)(2,1)}) custom-call(bf16[32,256]{1,0:T(8,128)(2,1)} %refs_0_.1, s32[8,32]{1,0:T(8,128)} %bitcast.17, f32[8,32]{1,0:T(8,128)} %bitcast.18, bf16[512,256]{1,0:T(8,128)(2,1)} %bitcast.16, ...), custom_call_target="tpu_custom_call" | custom-call | tf_op jit(solution)/shard_map/expert_backward/pallas_call | solution.py:439
  89.4 2.2 %hand_over.1 = (bf16[32,256]{1,0:T(8,128)(2,1)}, bf16[256,1024]{1,0:T(8,128)(2,1)}, bf16[256,1024]{1,0:T(8,128)(2,1)}, bf16[1024,256]{1,0:T(8,128)(2,1)}) custom-call(bf16[32,256]{1,0:T(8,128)(2,1)} %get-tuple-element.12.refs_0_, bf16[256,1024]{1,0:T(8,128)(2,1)} %get-tuple-element.13.refs_1_, bf16[256,1024]{1,0:T(8,128)(2,1)} %get-tuple-element.14.refs_2_, ...), custom_call_target="tpu_custom_call" | custom-call | tf_op jit(solution)/shard_map/hand_over/pallas_call | solution.py:506

commit v3 on v2

--- a/solution.py
+++ b/solution.py
@@ -346,7 +346,6 @@
     scatter(2)
     rs_start(2)
     leaves(3)
-    reduce(1)
     share(3).wait_recv()
     scatter(3)
     rs_start(3)
@@ -355,15 +354,18 @@
     local(0)
     reduce(2)
     join(0)
-    local(1)
     reduce(3)
-    join(1)
+    reduce(1)
     local(2)
     join(2)
     local(3)
-    forward(5, -5, 8, -8, 2, -2)
+    forward(2, -2)
     join(3)
-    forward(14, -14, 11, -11, 12, -12)
+    local(1)
+    forward(14, -14, 11, -11)
+    join(1)
+    forward(12, -12)
+    forward(5, -5, 8, -8)
 
     load_xin.wait()
     for i, o in enumerate(ORDER):

time: 92.8 us -> 89.4 us (0.963)
  Pallas kernels: 91 us -> 88 us
    pallas_call x1, Pallas kernels: 88.7 us -> 85.7 us  [on_device(): pl.pallas_call(lambda *refs: kernel(n_dp, n_z, *refs), out_shape=(jax.Sha...]
where the time goes in v3:
time: 89.4 us; the launch traced here: 88.6 us
  Pallas kernels  88 us (98%)
    pallas_call x1, Pallas kernels, on_device(): pl.pallas_call(lambda *refs: kernel(n_dp, n_z, *refs), out_shape=(jax.Sha...  85.7 us
    pallas_call x1, Pallas kernels, on_device(): pl.pallas_call(hand_over, out_shape=tuple((jax.ShapeDtypeStruct(a.shape,...  2.24 us

profile of v3, /device:TPU:6, one launch (start us, length us, event | category | flops | bytes accessed | tf_op | source)
XLA Modules:
  0.0 88.6 jit_solution(11460994951328983774)
XLA Ops:
  0.6 85.7 %expert_backward.1 = (bf16[32,256]{1,0:T(8,128)(2,1)}, bf16[256,1024]{1,0:T(8,128)(2,1)}, bf16[256,1024]{1,0:T(8,128)(2,1)}, bf16[1024,256]{1,0:T(8,128)(2,1)}) custom-call(bf16[32,256]{1,0:T(8,128)(2,1)} %refs_0_.1, s32[8,32]{1,0:T(8,128)} %bitcast.17, f32[8,32]{1,0:T(8,128)} %bitcast.18, bf16[512,256]{1,0:T(8,128)(2,1)} %bitcast.16, ...), custom_call_target="tpu_custom_call" | custom-call | tf_op jit(solution)/shard_map/expert_backward/pallas_call | solution.py:441
  86.4 2.2 %hand_over.1 = (bf16[32,256]{1,0:T(8,128)(2,1)}, bf16[256,1024]{1,0:T(8,128)(2,1)}, bf16[256,1024]{1,0:T(8,128)(2,1)}, bf16[1024,256]{1,0:T(8,128)(2,1)}) custom-call(bf16[32,256]{1,0:T(8,128)(2,1)} %get-tuple-element.12.refs_0_, bf16[256,1024]{1,0:T(8,128)(2,1)} %get-tuple-element.13.refs_1_, bf16[256,1024]{1,0:T(8,128)(2,1)} %get-tuple-element.14.refs_2_, ...), custom_call_target="tpu_custom_call" | custom-call | tf_op jit(solution)/shard_map/hand_over/pallas_call | solution.py:508
